TPU v7x, 128 devices: a whole 4x4x4 slice. The times are simulated.
128 devices in a mesh: tm: 8 (over x, core), sy: 4 (over z), sx: 4 (over y).
Axes of the slice: x: 4, y: 4, z: 4, core: 2. Of those that a mesh axis runs over, the one named last changes fastest.
Arguments:
- latent_init: float32 [64, 96, 320], P('sy', 'sx'), may hold values from -80 to 80
- step_noise: bfloat16 [32, 64, 96, 320], P('tm', 'sy', 'sx'), may hold values from -6 to 6
- coef_state: float32 [32], P('tm'), may hold values from -0.06 to -0.01
- coef_drift: float32 [32], P('tm'), may hold values from -0.1 to 0.1
- coef_noise: float32 [32], P('tm'), may hold values from 0.05 to 0.2
- step_index: int32 [32], P('tm'), may hold values from 0 to 999
- time_table: float32 [1000, 320], replicated, may hold values from -1.5 to 1.5
- norm_gain: float32 [320], replicated, may hold values from 0.25 to 1.75
- conv_weight: bfloat16 [3, 3, 320, 320], replicated, may hold values from -0.109375 to 0.109375
- reward_grad: float32 [64, 96, 320], P('sy', 'sx'), may hold values from -0.18 to 0.18
Outputs:
- trajectory: float32 [32, 64, 96, 320], P('tm', 'sy', 'sx')
- grad_weight: float32 [3, 3, 320, 320], P(None, None, None, 'tm')
All inputs are finite; a program needn't handle non-finite values.
Results may differ from a plain program's by a relative error of at most 0.0009.
The roundings to bfloat16 on the way count: a program that leaves them out, or rounds other values in their place, can miss the bound.
Values may be sent and summed in bfloat16 or wider, within the bound.
A program may use at most 128 MiB of HBM per device.

v0:
```python
import jax
import jax.numpy as jnp
from jax import lax
from jax.sharding import PartitionSpec as P

GROUPS = 32
ITERS = 2
EPSILON = 1e-05


def prefix(value, axis, join, neutral, backward):
    count, mine = (lax.axis_size(axis), lax.axis_index(axis))
    pieces = lax.all_gather(value, axis)
    if backward:
        pieces = pieces[::-1]
        mine = count - 1 - mine
    subtotal = jnp.full_like(value, 0) + jnp.asarray(neutral, value.dtype)

    def step(position, subtotal):
        longer = join(subtotal, pieces[position])
        return jnp.where(position < mine, longer, subtotal)

    return lax.fori_loop(0, count - 1, step, subtotal)


def with_halo(block, sides, width):
    for axis, dim in sides:
        count = lax.axis_size(axis)
        forward = [(i, i + 1) for i in range(count - 1)]
        backward = [(target, source) for source, target in forward]
        low = lax.ppermute(
            lax.slice_in_dim(block, block.shape[dim] - width, None, axis=dim), axis, forward
        )
        high = lax.ppermute(lax.slice_in_dim(block, 0, width, axis=dim), axis, backward)
        block = jnp.concatenate([low, block, high], axis=dim)
    return block


def add_terms(earlier, later):
    return earlier + later


def lower_total(block_total, reverse):
    return prefix(block_total, "tm", add_terms, jnp.zeros_like(block_total), reverse)


def group_count(tile_rows, tile_cols, channels):
    return tile_rows * lax.axis_size("sy") * tile_cols * lax.axis_size("sx") * (channels // GROUPS)


def group_stats(grouped, cell_count):
    totals = lax.psum(jnp.sum(grouped, axis=(1, 3)), ("sy", "sx"))
    center = totals / cell_count
    shifted = grouped - center[:, None, :, None]
    spread = lax.psum(jnp.sum(shifted * shifted, axis=(1, 3)), ("sy", "sx")) / cell_count
    return (shifted, spread)


def prepare(states, modulate):
    steps_here, tile_rows, tile_cols, channels = states.shape
    grouped = states.reshape(steps_here, tile_rows * tile_cols, GROUPS, channels // GROUPS)
    shifted, spread = group_stats(grouped, group_count(tile_rows, tile_cols, channels))
    inv_std = 1.0 / jnp.sqrt(spread + EPSILON)
    normal_field = (shifted * inv_std[:, None, :, None]).reshape(states.shape)
    pre_act = normal_field * modulate[:, None, None, :]
    activation = jax.nn.silu(pre_act).astype(jnp.bfloat16)
    act_pad = with_halo(activation, (("sy", 1), ("sx", 2)), 1)
    return (normal_field, inv_std, pre_act, act_pad)


def convolve(act_pad, conv_weight, tile_rows, tile_cols):
    result = jnp.zeros(
        act_pad.shape[:1] + (tile_rows, tile_cols, conv_weight.shape[3]), jnp.float32
    )
    for row_off in range(3):
        for col_off in range(3):
            window = act_pad[:, row_off : row_off + tile_rows, col_off : col_off + tile_cols, :]
            result = result + jnp.einsum(
                "bhwc,cd->bhwd",
                window,
                conv_weight[row_off, col_off],
                preferred_element_type=jnp.float32,
            )
    return result


def backprop(upstream, act_cache, modulate, conv_weight, need_state):
    normal_field, inv_std, pre_act, act_pad = act_cache
    steps_here, tile_rows, tile_cols, channels = upstream.shape
    up_half = upstream.astype(jnp.bfloat16)
    weight_rows = []
    for row_off in range(3):
        weight_cols = []
        for col_off in range(3):
            window = act_pad[:, row_off : row_off + tile_rows, col_off : col_off + tile_cols, :]
            weight_cols.append(
                jnp.einsum("bhwc,bhwd->cd", window, up_half, preferred_element_type=jnp.float32)
            )
        weight_rows.append(jnp.stack(weight_cols))
    grad_piece = jnp.stack(weight_rows)
    if not need_state:
        return (upstream, grad_piece)
    up_pad = with_halo(up_half, (("sy", 1), ("sx", 2)), 1)
    d_act = jnp.zeros(upstream.shape, jnp.float32)
    for row_off in range(3):
        for col_off in range(3):
            window = up_pad[
                :, 2 - row_off : 2 - row_off + tile_rows, 2 - col_off : 2 - col_off + tile_cols, :
            ]
            d_act = d_act + jnp.einsum(
                "bhwd,cd->bhwc",
                window,
                conv_weight[row_off, col_off],
                preferred_element_type=jnp.float32,
            )
    sig_value = jax.nn.sigmoid(pre_act)
    d_norm = d_act * sig_value * (1.0 + pre_act * (1.0 - sig_value)) * modulate[:, None, None, :]
    group_shape = (steps_here, tile_rows * tile_cols, GROUPS, channels // GROUPS)
    grouped_d = d_norm.reshape(group_shape)
    grouped_n = normal_field.reshape(group_shape)
    cell_count = group_count(tile_rows, tile_cols, channels)
    plain_sum, cross_sum = lax.psum(
        (jnp.sum(grouped_d, axis=(1, 3)), jnp.sum(grouped_d * grouped_n, axis=(1, 3))), ("sy", "sx")
    )
    plain_mean = plain_sum / cell_count
    cross_mean = cross_sum / cell_count
    d_group = (
        grouped_d - plain_mean[:, None, :, None] - grouped_n * cross_mean[:, None, :, None]
    ) * inv_std[:, None, :, None]
    return (upstream + d_group.reshape(upstream.shape), grad_piece)


def shards(
    latent_init,
    step_noise,
    coef_state,
    coef_drift,
    coef_noise,
    step_index,
    time_table,
    norm_gain,
    conv_weight,
    reward_grad,
):
    tile_rows, tile_cols = (step_noise.shape[1], step_noise.shape[2])
    table_ids = jnp.arange(time_table.shape[0], dtype=jnp.int32)
    one_hot = (step_index[:, None] == table_ids[None, :]).astype(jnp.float32)
    embedded = jnp.dot(one_hot, time_table, precision=lax.Precision.HIGHEST)
    modulate = norm_gain[None, :] * (1.0 + embedded)
    state_c = coef_state[:, None, None, None]
    drift_c = coef_drift[:, None, None, None]
    noise_c = coef_noise[:, None, None, None]
    states = jnp.broadcast_to(latent_init[None], step_noise.shape)
    saved_states = []
    caches = []
    trajectory = states
    for sweep_index in range(ITERS):
        saved_states.append(states)
        act_cache = prepare(states, modulate)
        caches.append(act_cache)
        drift_term = states + convolve(act_cache[3], conv_weight, tile_rows, tile_cols)
        increment = (
            state_c * states + drift_c * drift_term + noise_c * step_noise.astype(jnp.float32)
        )
        running = jnp.cumsum(increment, axis=0)
        offset = lower_total(running[-1], False)
        trajectory = latent_init[None] + (offset[None] + running)
        if sweep_index + 1 < ITERS:
            before = jnp.concatenate([jnp.zeros_like(running[:1]), running[:-1]], axis=0)
            states = latent_init[None] + (offset[None] + before)
    adjoint = jnp.broadcast_to(reward_grad[None], step_noise.shape)
    grad_total = jnp.zeros(conv_weight.shape, jnp.float32)
    for sweep_index in range(ITERS - 1, -1, -1):
        act_cache = prepare(saved_states[sweep_index], modulate)
        upstream = drift_c * adjoint
        d_state, grad_piece = backprop(upstream, act_cache, modulate, conv_weight, sweep_index > 0)
        grad_total = grad_total + grad_piece
        if sweep_index > 0:
            through = state_c * adjoint + d_state
            suffix = jnp.cumsum(through[::-1], axis=0)[::-1]
            higher = lower_total(suffix[0], True)
            after = jnp.concatenate([suffix[1:], jnp.zeros_like(suffix[:1])], axis=0)
            adjoint = higher[None] + after
    share = lax.psum_scatter(grad_total, "tm", scatter_dimension=3, tiled=True)
    grad_weight = lax.psum(share, ("sy", "sx"))
    return (trajectory, grad_weight)


def solution(mesh):
    placed = (
        P("sy", "sx", None),
        P("tm", "sy", "sx", None),
        P("tm"),
        P("tm"),
        P("tm"),
        P("tm"),
        P(),
        P(),
        P(),
        P("sy", "sx", None),
    )
    return jax.shard_map(
        shards,
        mesh=mesh,
        in_specs=placed,
        out_specs=(P("tm", "sy", "sx", None), P(None, None, None, "tm")),
        check_vma=False,
    )
```

profile of v0, /device:TPU:0, one launch (start us, length us, event | category | flops | bytes accessed | tf_op | source)
XLA Modules:
  0.0 634.3 jit_solution(18137577999258617183)
XLA Ops:
  8.7 42.0 %psum.46 = f32[4,32]{1,0:T(4,128)S(1)} all-reduce(f32[4,32]{1,0:T(4,128)S(1)} %reduce_sum.117), channel_id=1, replica_groups=mesh['tm'=8,'sy'=4,'sx'=4] {'sy','sx'}, use_global_device_ids=true, to_apply=%region_2.0 | all-reduce | flops 128 | bytes 1024 | tf_op jit(solution)/shard_map/psum | solution.py:52
  52.5 35.5 %psum.49 = f32[4,32]{1,0:T(4,128)S(1)} all-reduce(f32[4,32]{1,0:T(4,128)S(1)} %reduce_sum.120), channel_id=1, replica_groups=mesh['tm'=8,'sy'=4,'sx'=4] {'sy','sx'}, use_global_device_ids=true, to_apply=%region_5.6 | all-reduce | flops 128 | bytes 1024 | tf_op jit(solution)/shard_map/psum | solution.py:55
  98.3 3.9 collective-permute-start.2
  123.3 6.3 fusion.33
  135.9 3.3 fusion
  142.3 4.7 collective-permute-start.11
  147.1 3.3 fusion.48
  166.6 8.7 %while.42 = (s32[]{:T(128)}, f32[16,24,320]{2,1,0:T(8,128)S(1)}, s32[]{:T(128)}, f32[8,16,24,320]{3,2,1,0:T(8,128)}, s32[]{:T(128)}, /*index=5*/s32[]{:T(128)}) while((s32[]{:T(128)}, f32[16,24,320]{2,1,0:T(8,128)S(1)}, s32[]{:T(128)}, f32[8,16,24,320]{3,2,1,0:T(8,128)}, s32[]{:T(128)}, /*index=5*/s32[]{:T(128)}) %tuple.106), condition=%wide.region_8.9_spmd.clone, body=%wide.region_7.8_spmd.clone.sunk | while | flops 368644 | bytes 1474653 | solution.py:23
  177.3 39.5 %psum.50 = f32[4,32]{1,0:T(4,128)S(1)} all-reduce(f32[4,32]{1,0:T(4,128)S(1)} %reduce_sum.123), channel_id=1, replica_groups=mesh['tm'=8,'sy'=4,'sx'=4] {'sy','sx'}, use_global_device_ids=true, to_apply=%region_11.12 | all-reduce | flops 128 | bytes 1024 | tf_op jit(solution)/shard_map/psum | solution.py:52
  222.4 36.1 %psum.51 = f32[4,32]{1,0:T(4,128)} all-reduce(f32[4,32]{1,0:T(4,128)} %reduce_sum.126), channel_id=1, replica_groups=mesh['tm'=8,'sy'=4,'sx'=4] {'sy','sx'}, use_global_device_ids=true, to_apply=%region_14.15 | all-reduce | flops 128 | bytes 1024 | tf_op jit(solution)/shard_map/psum | solution.py:55
  261.5 11.5 %fusion.219 = (f32[4,320]{1,0:T(4,128)}, f32[4,320]{1,0:T(4,128)}, f32[4,16,24,320]{3,2,1,0:T(8,128)}) fusion(f32[4,320]{1,0:T(4,128)} %mul.201, f32[4,320]{1,0:T(4,128)S(1)} %sub.66, f32[3,16,24,320]{3,2,1,0:T(8,128)S(1)} %slice.280, f32[16,24,320]{2,1,0:T(8,128)S(1)} %get-tuple-element.239, f32[16,24,320]{2,1,0:T(8,128)S(1)} %copy-done.2, ...), kind=kOutput, calls=%fused_computation.276 | convolution fusion | flops 326858240 | bytes 24750080 | tf_op jit(solution)/shard_map/bhwd,cd->bhwc/dot_general | solution.py:110
  278.9 38.4 %all-reduce.3 = (f32[4,32]{1,0:T(4,128)}, f32[4,32]{1,0:T(4,128)}) all-reduce(f32[4,32]{1,0:T(4,128)} %reduce_sum.132, f32[4,32]{1,0:T(4,128)} %reduce_sum.129), channel_id=1, replica_groups=mesh['tm'=8,'sy'=4,'sx'=4] {'sy','sx'}, use_global_device_ids=true, to_apply=%region_23.24 | all-reduce | flops 256 | bytes 2048 | tf_op jit(solution)/shard_map/psum | solution.py:122
  323.7 5.2 fusion.18
  328.9 3.3 rev.7
  344.5 3.5 fusion.162
  356.8 3.8 fusion.146
  363.9 3.3 fusion.145
  378.1 3.4 fusion.110
  381.5 4.9 rev.8
  386.4 8.7 %while.44 = (s32[]{:T(128)}, f32[16,24,320]{2,1,0:T(8,128)S(1)}, s32[]{:T(128)}, f32[8,16,24,320]{3,2,1,0:T(8,128)}, s32[]{:T(128)}, /*index=5*/s32[]{:T(128)}) while((s32[]{:T(128)}, f32[16,24,320]{2,1,0:T(8,128)S(1)}, s32[]{:T(128)}, f32[8,16,24,320]{3,2,1,0:T(8,128)}, s32[]{:T(128)}, /*index=5*/s32[]{:T(128)}) %tuple.112), condition=%wide.region_26.27_spmd.clone, body=%wide.region_25.26_spmd.clone.sunk | while | flops 368644 | bytes 1474653 | solution.py:23
  410.1 8.4 %copy.14 = f32[3,3,320,320]{2,1,0,3:T(4,128)} copy(f32[3,3,320,320]{3,2,1,0:T(8,128)} %maximum_add_fusion) | data formatting | bytes 7372800 | tf_op jit(solution)/shard_map/add | solution.py:177
  419.1 3.9 fusion.113
  423.0 3.6 fusion.116
  426.6 3.4 fusion.119
  430.0 3.5 fusion.122
  433.5 3.4 fusion.125
  436.9 8.6 %fusion.19 = f32[4,16,24,320]{3,2,1,0:T(8,128)S(1)} fusion(f32[4,16,24,320]{3,2,1,0:T(8,128)} %fusion.110, f32[4,16,24,320]{3,2,1,0:T(8,128)} %fusion.145, f32[4,16,24,320]{3,2,1,0:T(8,128)} %fusion.113, f32[4,16,24,320]{3,2,1,0:T(8,128)} %fusion.116, f32[4,16,24,320]{3,2,1,0:T(8,128)} %fusion.162, f32[4,16,24,320]{3,2,1,0:T(8,128)} %fusion.119, ...), kind=kOutput, calls=%fused_computation.31 | output fusion | flops 9830400 | bytes 23101488 | tf_op jit(solution)/shard_map/jit(cumsum)/reduce_window_sum | solution.py:165
  449.1 50.9 %all-reduce.9.cloned.1.call-done = f32[3,3,320,320]{2,1,0,3:T(4,128)} async-done(((f32[3,3,320,320]{2,1,0,3:T(4,128)}), f32[3,3,320,320]{2,1,0,3:T(4,128)}) %all-reduce.9.cloned.1.call-update) | async-done | bytes 3686416
  502.2 33.7 %all-gather.6.cloned.1.call-done = f32[8,16,24,320]{3,2,1,0:T(8,128)} async-done(((f32[1,16,24,320]{3,2,1,0:T(8,128)}), f32[8,16,24,320]{3,2,1,0:T(8,128)}) %all-gather.6.cloned.1.call-update) | async-done | bytes 3932176 | tf_op jit(solution)/shard_map/all_gather | solution.py:13
  535.9 8.7 %while.43 = (s32[]{:T(128)}, f32[16,24,320]{2,1,0:T(8,128)S(1)}, s32[]{:T(128)}, f32[8,16,24,320]{3,2,1,0:T(8,128)}, s32[]{:T(128)}, /*index=5*/s32[]{:T(128)}) while((s32[]{:T(128)}, f32[16,24,320]{2,1,0:T(8,128)S(1)}, s32[]{:T(128)}, f32[8,16,24,320]{3,2,1,0:T(8,128)}, s32[]{:T(128)}, /*index=5*/s32[]{:T(128)}) %tuple.109), condition=%wide.region_17.18_spmd.clone, body=%wide.region_16.17_spmd.clone.sunk | while | flops 368644 | bytes 1474653 | solution.py:23
  544.6 3.4 add_add_fusion
  548.0 77.7 %all-reduce.7.cloned.1.call-done = f32[3,3,320,40]{2,1,0,3:T(4,128)} async-done(((f32[3,3,320,40]{2,1,0,3:T(4,128)}), f32[3,3,320,40]{2,1,0,3:T(4,128)}) %all-reduce.7.cloned.1.call-update) | async-done | bytes 460816 | tf_op jit(solution)/shard_map/psum | solution.py:185
  (255 shorter events, 166.0 us)
Async XLA Ops:
  7.2 81.0 %copy-start = (f32[1000,320]{0,1:T(8,128)S(1)}, f32[1000,320]{0,1:T(8,128)}, u32[]{:S(2)}) copy-start(f32[1000,320]{0,1:T(8,128)} %param.22) | copy-start | bytes 3840004
  7.2 82.6 %copy-start.2 = (f32[16,24,320]{2,1,0:T(8,128)S(1)}, f32[16,24,320]{2,1,0:T(8,128)}, u32[]{:S(2)}) copy-start(f32[16,24,320]{2,1,0:T(8,128)} %param.16) | copy-start | bytes 1474564
  7.2 159.4 %all-gather.4.cloned.1.call-start = ((), (), s32[]{:S(2)}) async-start(), calls=%async_computation | async-start | bytes 5308416 | tf_op jit(solution)/shard_map/all_gather | solution.py:13
  51.0 44.8 %copy-start.39 = (f32[4,320]{1,0:T(4,128)}, f32[4,320]{1,0:T(4,128)S(1)}, u32[]{:S(2)}) copy-start(f32[4,320]{1,0:T(4,128)S(1)} %sub.62) | copy-start | bytes 15364
  90.5 18.4 %copy-start.5 = (bf16[4,16,24,320]{3,2,1,0:T(8,128)(2,1)}, bf16[4,16,24,320]{3,2,1,0:T(8,128)(2,1)S(1)}, u32[]{:S(2)}) copy-start(bf16[4,16,24,320]{3,2,1,0:T(8,128)(2,1)S(1)} %fusion.17) | copy-start | bytes 2949124
  90.5 5.2 collective-permute-start
  91.8 6.2 collective-permute-start.1
  95.8 13.1 %copy-start.32 = (bf16[4,1,24,320]{3,2,1,0:T(8,128)(2,1)}, bf16[4,1,24,320]{3,2,1,0:T(8,128)(2,1)S(1)}, u32[]{:S(2)}) copy-start(bf16[4,1,24,320]{3,2,1,0:T(8,128)(2,1)S(1)} %collective-permute-done) | copy-start | bytes 184324
  98.1 10.8 %copy-start.30 = (bf16[4,1,24,320]{3,2,1,0:T(8,128)(2,1)}, bf16[4,1,24,320]{3,2,1,0:T(8,128)(2,1)S(1)}, u32[]{:S(2)}) copy-start(bf16[4,1,24,320]{3,2,1,0:T(8,128)(2,1)S(1)} %collective-permute-done.1) | copy-start | bytes 184324
  98.3 7.8 %collective-permute-start.2 = (bf16[4,18,1,320]{3,2,1,0:T(2,128)(2,1)S(1)}, bf16[4,18,1,320]{3,2,1,0:T(2,128)(2,1)S(1)}, u32[]{:S(2)}, u32[]{:S(2)}) collective-permute-start(bf16[4,18,1,320]{3,2,1,0:T(2,128)(2,1)S(1)} %get-tuple-element.333), channel_id=1, source_target_pairs={{0,1},{1,2},{2,3},{4,5},{5,6},{6,7},{8,9},{9,10},{10,11},{12,13},{... | collective-permute-start | bytes 138248 | tf_op jit(solution)/shard_map/ppermute | solution.py:31
  102.2 6.6 %collective-permute-start.3 = (bf16[4,18,1,320]{3,2,1,0:T(2,128)(2,1)S(1)}, bf16[4,18,1,320]{3,2,1,0:T(2,128)(2,1)S(1)}, u32[]{:S(2)}, u32[]{:S(2)}) collective-permute-start(bf16[4,18,1,320]{3,2,1,0:T(2,128)(2,1)S(1)} %get-tuple-element.334), channel_id=1, source_target_pairs={{1,0},{2,1},{3,2},{5,4},{6,5},{7,6},{9,8},{10,9},{11,10},{13,12},{... | collective-permute-start | bytes 138248 | tf_op jit(solution)/shard_map/ppermute | solution.py:34
  110.0 10.8 %copy-start.13 = (bf16[4,18,25,320]{3,2,1,0:T(8,128)(2,1)}, bf16[4,18,25,320]{3,2,1,0:T(8,128)(2,1)S(1)}, u32[]{:S(2)}) copy-start(bf16[4,18,25,320]{3,2,1,0:T(8,128)(2,1)S(1)} %get-tuple-element.331) | copy-start | bytes 3456004
  123.3 8.7 %copy-start.28 = (f32[16,24,320]{2,1,0:T(8,128)S(1)}, f32[16,24,320]{2,1,0:T(8,128)}, u32[]{:S(2)}) copy-start(f32[16,24,320]{2,1,0:T(8,128)} %param.25) | copy-start | bytes 1474564
  131.9 249.6 %all-gather.8.cloned.1.call-start = ((), (), s32[]{:S(2)}) async-start(), calls=%async_computation.2 | async-start | bytes 5308416 | tf_op jit(solution)/shard_map/all_gather | solution.py:13
  132.3 18.0 %copy-start.7 = (bf16[4,16,24,320]{3,2,1,0:T(8,128)(2,1)}, bf16[4,16,24,320]{3,2,1,0:T(8,128)(2,1)S(1)}, u32[]{:S(2)}) copy-start(bf16[4,16,24,320]{3,2,1,0:T(8,128)(2,1)S(1)} %multiply_convert_fusion) | copy-start | bytes 2949124
  132.3 6.9 %collective-permute-start.8 = (bf16[4,1,24,320]{3,2,1,0:T(8,128)(2,1)S(1)}, bf16[4,1,24,320]{3,2,1,0:T(8,128)(2,1)S(1)}, u32[]{:S(2)}, u32[]{:S(2)}) collective-permute-start(bf16[4,1,24,320]{3,2,1,0:T(8,128)(2,1)S(1)} %get-tuple-element.336), channel_id=1, source_target_pairs={{0,4},{4,8},{8,12},{1,5},{5,9},{9,13},{2,6},{6,10},{10,14},{3,7},{... | collective-permute-start | bytes 184328 | tf_op jit(solution)/shard_map/ppermute | solution.py:31
  134.6 6.2 collective-permute-start.9
  139.2 11.1 %copy-start.10 = (bf16[3,3,320,320]{3,2,1,0:T(8,128)(2,1)S(1)}, bf16[3,3,320,320]{3,2,1,0:T(8,128)(2,1)}, u32[]{:S(2)}) copy-start(bf16[3,3,320,320]{3,2,1,0:T(8,128)(2,1)} %param.24) | copy-start | bytes 5529604
  139.2 11.1 %copy-start.34 = (bf16[4,1,24,320]{3,2,1,0:T(8,128)(2,1)}, bf16[4,1,24,320]{3,2,1,0:T(8,128)(2,1)S(1)}, u32[]{:S(2)}) copy-start(bf16[4,1,24,320]{3,2,1,0:T(8,128)(2,1)S(1)} %collective-permute-done.8) | copy-start | bytes 184324
  140.8 9.5 %copy-start.36 = (bf16[4,1,24,320]{3,2,1,0:T(8,128)(2,1)}, bf16[4,1,24,320]{3,2,1,0:T(8,128)(2,1)S(1)}, u32[]{:S(2)}) copy-start(bf16[4,1,24,320]{3,2,1,0:T(8,128)(2,1)S(1)} %collective-permute-done.9) | copy-start | bytes 184324
  141.0 11.8 %collective-permute-start.10 = (bf16[4,18,1,320]{3,2,1,0:T(2,128)(2,1)S(1)}, bf16[4,18,1,320]{3,2,1,0:T(2,128)(2,1)S(1)}, u32[]{:S(2)}, u32[]{:S(2)}) collective-permute-start(bf16[4,18,1,320]{3,2,1,0:T(2,128)(2,1)S(1)} %get-tuple-element.326), channel_id=1, source_target_pairs={{1,0},{2,1},{3,2},{5,4},{6,5},{7,6},{9,8},{10,9},{11,10},{13,12},{... | collective-permute-start | bytes 138248 | tf_op jit(solution)/shard_map/ppermute | solution.py:34
  142.3 10.5 %collective-permute-start.11 = (bf16[4,18,1,320]{3,2,1,0:T(2,128)(2,1)S(1)}, bf16[4,18,1,320]{3,2,1,0:T(2,128)(2,1)S(1)}, u32[]{:S(2)}, u32[]{:S(2)}) collective-permute-start(bf16[4,18,1,320]{3,2,1,0:T(2,128)(2,1)S(1)} %get-tuple-element.325), channel_id=1, source_target_pairs={{0,1},{1,2},{2,3},{4,5},{5,6},{6,7},{8,9},{9,10},{10,11},{12,13},{... | collective-permute-start | bytes 138248 | tf_op jit(solution)/shard_map/ppermute | solution.py:31
  332.1 9.1 %copy-start.44 = (f32[4]{0:T(128)S(1)}, f32[4]{0:T(128)}, u32[]{:S(2)}) copy-start(f32[4]{0:T(128)} %param.19) | copy-start | bytes 52
  336.3 163.8 %all-reduce.9.cloned.1.call-start = ((), (), s32[]{:S(2)}) async-start(), calls=%async_computation.4 | async-start | bytes 11796480
  337.9 14.2 %collective-permute-start.4 = (bf16[4,1,24,320]{3,2,1,0:T(8,128)(2,1)}, bf16[4,1,24,320]{3,2,1,0:T(8,128)(2,1)}, u32[]{:S(2)}, u32[]{:S(2)}) collective-permute-start(bf16[4,1,24,320]{3,2,1,0:T(8,128)(2,1)} %get-tuple-element.337), channel_id=1, source_target_pairs={{0,4},{4,8},{8,12},{1,5},{5,9},{9,13},{2,6},{6,10},{10,14},{3,7},{... | collective-permute-start | bytes 184328 | tf_op jit(solution)/shard_map/ppermute | solution.py:31
  339.8 12.3 %collective-permute-start.5 = (bf16[4,1,24,320]{3,2,1,0:T(8,128)(2,1)}, bf16[4,1,24,320]{3,2,1,0:T(8,128)(2,1)}, u32[]{:S(2)}, u32[]{:S(2)}) collective-permute-start(bf16[4,1,24,320]{3,2,1,0:T(8,128)(2,1)} %get-tuple-element.338), channel_id=1, source_target_pairs={{4,0},{8,4},{12,8},{5,1},{9,5},{13,9},{6,2},{10,6},{14,10},{7,3},{... | collective-permute-start | bytes 184328 | tf_op jit(solution)/shard_map/ppermute | solution.py:34
  353.7 13.6 %collective-permute-start.6 = (bf16[4,18,1,320]{3,2,1,0:T(2,128)(2,1)S(1)}, bf16[4,18,1,320]{3,2,1,0:T(2,128)(2,1)S(1)}, u32[]{:S(2)}, u32[]{:S(2)}) collective-permute-start(bf16[4,18,1,320]{3,2,1,0:T(2,128)(2,1)S(1)} %get-tuple-element.329), channel_id=1, source_target_pairs={{0,1},{1,2},{2,3},{4,5},{5,6},{6,7},{8,9},{9,10},{10,11},{12,13},{... | collective-permute-start | bytes 138248 | tf_op jit(solution)/shard_map/ppermute | solution.py:31
  355.5 11.8 %collective-permute-start.7 = (bf16[4,18,1,320]{3,2,1,0:T(2,128)(2,1)S(1)}, bf16[4,18,1,320]{3,2,1,0:T(2,128)(2,1)S(1)}, u32[]{:S(2)}, u32[]{:S(2)}) collective-permute-start(bf16[4,18,1,320]{3,2,1,0:T(2,128)(2,1)S(1)} %get-tuple-element.330), channel_id=1, source_target_pairs={{1,0},{2,1},{3,2},{5,4},{6,5},{7,6},{9,8},{10,9},{11,10},{13,12},{... | collective-permute-start | bytes 138248 | tf_op jit(solution)/shard_map/ppermute | solution.py:34
  418.5 117.4 %all-gather.6.cloned.1.call-start = ((), (), s32[]{:S(2)}) async-start(), calls=%async_computation.1 | async-start | bytes 5308416 | tf_op jit(solution)/shard_map/all_gather | solution.py:13
  436.9 11.0 %copy-start.49 = (u32[128]{0:T(128)S(1)}, u32[128]{0:T(128)}, u32[]{:S(2)}) copy-start(u32[128]{0:T(128)} %constant.115) | copy-start | bytes 1540
  447.8 177.9 %all-reduce.7.cloned.1.call-start = ((), (), s32[]{:S(2)}) async-start(), calls=%async_computation.3 | async-start | bytes 1474560 | tf_op jit(solution)/shard_map/psum | solution.py:185
  544.6 83.0 %copy-start.1 = (f32[1000,320]{0,1:T(8,128)S(1)}, f32[1000,320]{0,1:T(8,128)}, u32[]{:S(2)}) copy-start(f32[1000,320]{0,1:T(8,128)} %param.22) | copy-start | bytes 3840004
  (35 other events, 114.0 us)
Sparse Core Ops, SparseCore 0:
  132.0 33.4 all-gather.3
  336.4 29.2 all-gather.7
  418.7 81.3 all-reduce.8
  501.7 34.1 all-gather.5
  539.4 86.2 all-reduce.6
where the time goes:
time: 641 us; the launch traced here: 634 us
  blocking collectives  191 us (30%)
  waiting for transfers between devices  169 us (26%)
  matrix products  101 us (16%)
  other arithmetic  78.4 us (12%)
  local copies, waits for them, and re-layouts  53.7 us (8%)
  starting transfers between devices  24.9 us (4%)
  between operations  15.4 us (2%)
    psum x2, blocking collectives, group_stats(): totals = lax.psum(jnp.sum(grouped, axis=(1, 3)), ('sy', 'sx'))  81.5 us
    psum x1, waiting for transfers between devices, shards(): grad_weight = lax.psum(share, ('sy', 'sx'))  77.7 us
    psum x2, blocking collectives, group_stats(): lax.psum(jnp.sum(shifted * shifted, axis=(1, 3)), ('sy', 'sx')) / cell_count  71.6 us
    unnamed x6, waiting for transfers between devices  51 us
    dot_general x18, matrix products, convolve(): jnp.einsum('bhwc,cd->bhwd', window, conv_weight[row_off, col_off], prefer...  49.6 us
    psum x1, blocking collectives, backprop(): lax.psum((jnp.sum(grouped_d, axis=(1, 3)), jnp.sum(grouped_d * grouped_n,...  38.4 us
    all_gather x3, waiting for transfers between devices, prefix(): pieces = lax.all_gather(value, axis)  33.7 us
    dot_general x9, matrix products, backprop(): jnp.einsum('bhwd,cd->bhwc', window, conv_weight[row_off, col_off], prefer...  31.9 us
  transfers between devices with their start and end apart: 17, of which 6 were waited for; matrix products, arithmetic and copies ran while one was open for 17% of the time, Pallas kernels for 0%

commit v1 on v0

--- a/solution.py
+++ b/solution.py
@@ -52,7 +52,7 @@
     totals = lax.psum(jnp.sum(grouped, axis=(1, 3)), ("sy", "sx"))
     center = totals / cell_count
     shifted = grouped - center[:, None, :, None]
-    spread = lax.psum(jnp.sum(shifted * shifted, axis=(1, 3)), ("sy", "sx")) / cell_count
+    spread = lax.psum(lax.psum(jnp.sum(shifted * shifted, axis=(1, 3)), "sx"), "sy") / cell_count
     return (shifted, spread)
 
 

time: 641 us -> 605 us (0.944)
  blocking collectives: 191 us -> 153 us
    psum x2 -> x4, blocking collectives: 71.6 us -> 32.9 us  [the longest x2 16.7 us: group_stats(): lax.psum(lax.psum(jnp.sum(shifted * shifted, axis=(1, 3)), 'sx'), 'sy')]
  transfers between devices with their start and end apart: 17 -> 17, of which waited for: 6 -> 6; matrix products, arithmetic and copies ran while one was open for 17% -> 18% of each run, Pallas kernels for 0% -> 0%
where the time goes in v1:
time: 605 us; the launch traced here: 598 us
  waiting for transfers between devices  170 us (28%)
  blocking collectives  153 us (25%)
  matrix products  101 us (17%)
  other arithmetic  78.5 us (13%)
  local copies, waits for them, and re-layouts  53.6 us (9%)
  starting transfers between devices  26.5 us (4%)
  between operations  15.5 us (3%)
    psum x2, blocking collectives, group_stats(): totals = lax.psum(jnp.sum(grouped, axis=(1, 3)), ('sy', 'sx'))  80.4 us
    psum x1, waiting for transfers between devices, shards(): grad_weight = lax.psum(share, ('sy', 'sx'))  77.7 us
    unnamed x6, waiting for transfers between devices  51.7 us
    dot_general x18, matrix products, convolve(): jnp.einsum('bhwc,cd->bhwd', window, conv_weight[row_off, col_off], prefer...  49.5 us
    psum x1, blocking collectives, backprop(): lax.psum((jnp.sum(grouped_d, axis=(1, 3)), jnp.sum(grouped_d * grouped_n,...  39.5 us
    all_gather x3, waiting for transfers between devices, prefix(): pieces = lax.all_gather(value, axis)  33.7 us
    dot_general x9, matrix products, backprop(): jnp.einsum('bhwd,cd->bhwc', window, conv_weight[row_off, col_off], prefer...  31.9 us
    select_n x21, other arithmetic, step(): return jnp.where(position < mine, longer, subtotal)  25.6 us
  transfers between devices with their start and end apart: 17, of which 6 were waited for; matrix products, arithmetic and copies ran while one was open for 18% of the time, Pallas kernels for 0%

profile of v1, /device:TPU:0, one launch (start us, length us, event | category | flops | bytes accessed | tf_op | source)
XLA Modules:
  0.0 597.8 jit_solution(4228413107425633821)
XLA Ops:
  8.7 42.0 %psum.60 = f32[4,32]{1,0:T(4,128)S(1)} all-reduce(f32[4,32]{1,0:T(4,128)S(1)} %reduce_sum.117), channel_id=1, replica_groups=mesh['tm'=8,'sy'=4,'sx'=4] {'sy','sx'}, use_global_device_ids=true, to_apply=%region_2.0 | all-reduce | flops 128 | bytes 1024 | tf_op jit(solution)/shard_map/psum | solution.py:52
  52.5 7.7 %psum.61 = f32[4,32]{1,0:T(4,128)S(1)} all-reduce(f32[4,32]{1,0:T(4,128)S(1)} %reduce_sum.120), channel_id=1, replica_groups=mesh['tm'=8,'sy'=4,'sx'=4] {'sx'}, use_global_device_ids=true, to_apply=%region_5.6 | all-reduce | flops 128 | bytes 1024 | tf_op jit(solution)/shard_map/psum | solution.py:55
  60.3 8.0 %psum.64 = f32[4,32]{1,0:T(4,128)S(1)} all-reduce(f32[4,32]{1,0:T(4,128)S(1)} %psum.61), channel_id=1, replica_groups=mesh['tm'=8,'sy'=4,'sx'=4] {'sy'}, use_global_device_ids=true, to_apply=%region_6.7 | all-reduce | flops 128 | bytes 1024 | tf_op jit(solution)/shard_map/psum | solution.py:55
  70.8 3.6 collective-permute-start
  80.9 3.9 collective-permute-start.2
  105.9 6.3 %fusion.33 = f32[4,16,24,320]{3,2,1,0:T(8,128)S(1)} fusion(bf16[4,16,24,320]{3,2,1,0:T(8,128)(2,1)} %param.17, f32[4,16,24,320]{3,2,1,0:T(8,128)S(1)} %fusion.128, f32[4,16,24,320]{3,2,1,0:T(8,128)S(1)} %fusion.147, f32[4,16,24,320]{3,2,1,0:T(8,128)} %fusion.131, f32[4,16,24,320]{3,2,1,0:T(8,128)} %fusion.134, f32[4,16,24,320]{3,2,1,0:T(8,128)} %fusion.164, ...), kind=kOutput, calls=%fused_computation.49 | output fusion | flops 8847360 | bytes 21135408 | tf_op jit(solution)/shard_map/jit(cumsum)/reduce_window_sum | solution.py:165
  125.0 4.7 collective-permute-start.11
  149.2 8.7 %while.42 = (s32[]{:T(128)}, f32[16,24,320]{2,1,0:T(8,128)S(1)}, s32[]{:T(128)}, f32[8,16,24,320]{3,2,1,0:T(8,128)}, s32[]{:T(128)}, /*index=5*/s32[]{:T(128)}) while((s32[]{:T(128)}, f32[16,24,320]{2,1,0:T(8,128)S(1)}, s32[]{:T(128)}, f32[8,16,24,320]{3,2,1,0:T(8,128)}, s32[]{:T(128)}, /*index=5*/s32[]{:T(128)}) %tuple.106), condition=%wide.region_9.10_spmd.clone, body=%wide.region_8.9_spmd.clone.sunk | while | flops 368644 | bytes 1474653 | solution.py:23
  159.8 38.4 %psum.65 = f32[4,32]{1,0:T(4,128)S(1)} all-reduce(f32[4,32]{1,0:T(4,128)S(1)} %reduce_sum.123), channel_id=1, replica_groups=mesh['tm'=8,'sy'=4,'sx'=4] {'sy','sx'}, use_global_device_ids=true, to_apply=%region_12.13 | all-reduce | flops 128 | bytes 1024 | tf_op jit(solution)/shard_map/psum | solution.py:52
  203.9 8.4 %psum.66 = f32[4,32]{1,0:T(4,128)} all-reduce(f32[4,32]{1,0:T(4,128)} %reduce_sum.126), channel_id=1, replica_groups=mesh['tm'=8,'sy'=4,'sx'=4] {'sx'}, use_global_device_ids=true, to_apply=%region_15.16 | all-reduce | flops 128 | bytes 1024 | tf_op jit(solution)/shard_map/psum | solution.py:55
  212.3 8.7 %psum.69 = f32[4,32]{1,0:T(4,128)} all-reduce(f32[4,32]{1,0:T(4,128)} %psum.66), channel_id=1, replica_groups=mesh['tm'=8,'sy'=4,'sx'=4] {'sy'}, use_global_device_ids=true, to_apply=%region_16.17 | all-reduce | flops 128 | bytes 1024 | tf_op jit(solution)/shard_map/psum | solution.py:55
  224.0 11.5 %fusion.219 = (f32[4,320]{1,0:T(4,128)}, f32[4,320]{1,0:T(4,128)}, f32[4,16,24,320]{3,2,1,0:T(8,128)}) fusion(f32[4,320]{1,0:T(4,128)} %mul.201, f32[4,320]{1,0:T(4,128)S(1)} %sub.66, f32[3,16,24,320]{3,2,1,0:T(8,128)S(1)} %slice.280, f32[16,24,320]{2,1,0:T(8,128)S(1)} %get-tuple-element.239, f32[16,24,320]{2,1,0:T(8,128)S(1)} %copy-done.2, ...), kind=kOutput, calls=%fused_computation.276 | convolution fusion | flops 326858240 | bytes 24750080 | tf_op jit(solution)/shard_map/bhwd,cd->bhwc/dot_general | solution.py:110
  241.3 39.5 %all-reduce.3 = (f32[4,32]{1,0:T(4,128)}, f32[4,32]{1,0:T(4,128)}) all-reduce(f32[4,32]{1,0:T(4,128)} %reduce_sum.132, f32[4,32]{1,0:T(4,128)} %reduce_sum.129), channel_id=1, replica_groups=mesh['tm'=8,'sy'=4,'sx'=4] {'sy','sx'}, use_global_device_ids=true, to_apply=%region_25.26 | all-reduce | flops 256 | bytes 2048 | tf_op jit(solution)/shard_map/psum | solution.py:122
  287.3 5.2 fusion.18
  308.2 3.5 fusion.162
  319.9 3.8 fusion.146
  327.0 3.4 fusion.145
  341.4 3.4 fusion.110
  344.8 4.9 rev.8
  349.7 8.7 %while.44 = (s32[]{:T(128)}, f32[16,24,320]{2,1,0:T(8,128)S(1)}, s32[]{:T(128)}, f32[8,16,24,320]{3,2,1,0:T(8,128)}, s32[]{:T(128)}, /*index=5*/s32[]{:T(128)}) while((s32[]{:T(128)}, f32[16,24,320]{2,1,0:T(8,128)S(1)}, s32[]{:T(128)}, f32[8,16,24,320]{3,2,1,0:T(8,128)}, s32[]{:T(128)}, /*index=5*/s32[]{:T(128)}) %tuple.112), condition=%wide.region_28.29_spmd.clone, body=%wide.region_27.28_spmd.clone.sunk | while | flops 368644 | bytes 1474653 | solution.py:23
  373.3 8.4 %copy.14 = f32[3,3,320,320]{2,1,0,3:T(4,128)} copy(f32[3,3,320,320]{3,2,1,0:T(8,128)} %maximum_add_fusion) | data formatting | bytes 7372800 | tf_op jit(solution)/shard_map/add | solution.py:177
  382.0 3.9 fusion.113
  385.9 3.5 fusion.116
  389.4 3.4 fusion.119
  392.8 3.5 fusion.122
  396.3 3.4 fusion.125
  399.7 8.6 %fusion.19 = f32[4,16,24,320]{3,2,1,0:T(8,128)S(1)} fusion(f32[4,16,24,320]{3,2,1,0:T(8,128)} %fusion.110, f32[4,16,24,320]{3,2,1,0:T(8,128)} %fusion.145, f32[4,16,24,320]{3,2,1,0:T(8,128)} %fusion.113, f32[4,16,24,320]{3,2,1,0:T(8,128)} %fusion.116, f32[4,16,24,320]{3,2,1,0:T(8,128)} %fusion.162, f32[4,16,24,320]{3,2,1,0:T(8,128)} %fusion.119, ...), kind=kOutput, calls=%fused_computation.31 | output fusion | flops 9830400 | bytes 23101488 | tf_op jit(solution)/shard_map/jit(cumsum)/reduce_window_sum | solution.py:165
  411.9 51.7 %all-reduce.9.cloned.1.call-done = f32[3,3,320,320]{2,1,0,3:T(4,128)} async-done(((f32[3,3,320,320]{2,1,0,3:T(4,128)}), f32[3,3,320,320]{2,1,0,3:T(4,128)}) %all-reduce.9.cloned.1.call-update) | async-done | bytes 3686416
  465.7 33.7 %all-gather.6.cloned.1.call-done = f32[8,16,24,320]{3,2,1,0:T(8,128)} async-done(((f32[1,16,24,320]{3,2,1,0:T(8,128)}), f32[8,16,24,320]{3,2,1,0:T(8,128)}) %all-gather.6.cloned.1.call-update) | async-done | bytes 3932176 | tf_op jit(solution)/shard_map/all_gather | solution.py:13
  499.4 8.7 %while.43 = (s32[]{:T(128)}, f32[16,24,320]{2,1,0:T(8,128)S(1)}, s32[]{:T(128)}, f32[8,16,24,320]{3,2,1,0:T(8,128)}, s32[]{:T(128)}, /*index=5*/s32[]{:T(128)}) while((s32[]{:T(128)}, f32[16,24,320]{2,1,0:T(8,128)S(1)}, s32[]{:T(128)}, f32[8,16,24,320]{3,2,1,0:T(8,128)}, s32[]{:T(128)}, /*index=5*/s32[]{:T(128)}) %tuple.109), condition=%wide.region_19.20_spmd.clone, body=%wide.region_18.19_spmd.clone.sunk | while | flops 368644 | bytes 1474653 | solution.py:23
  508.1 3.4 add_add_fusion
  511.4 77.7 %all-reduce.7.cloned.1.call-done = f32[3,3,320,40]{2,1,0,3:T(4,128)} async-done(((f32[3,3,320,40]{2,1,0,3:T(4,128)}), f32[3,3,320,40]{2,1,0,3:T(4,128)}) %all-reduce.7.cloned.1.call-update) | async-done | bytes 460816 | tf_op jit(solution)/shard_map/psum | solution.py:185
  (257 shorter events, 173.8 us)
Async XLA Ops:
  7.2 61.3 %copy-start = (f32[1000,320]{0,1:T(8,128)S(1)}, f32[1000,320]{0,1:T(8,128)}, u32[]{:S(2)}) copy-start(f32[1000,320]{0,1:T(8,128)} %param.22) | copy-start | bytes 3840004
  7.2 62.9 %copy-start.2 = (f32[16,24,320]{2,1,0:T(8,128)S(1)}, f32[16,24,320]{2,1,0:T(8,128)}, u32[]{:S(2)}) copy-start(f32[16,24,320]{2,1,0:T(8,128)} %param.16) | copy-start | bytes 1474564
  7.2 142.0 %all-gather.4.cloned.1.call-start = ((), (), s32[]{:S(2)}) async-start(), calls=%async_computation | async-start | bytes 5308416 | tf_op jit(solution)/shard_map/all_gather | solution.py:13
  51.0 27.4 %copy-start.39 = (f32[4,320]{1,0:T(4,128)}, f32[4,320]{1,0:T(4,128)S(1)}, u32[]{:S(2)}) copy-start(f32[4,320]{1,0:T(4,128)S(1)} %sub.62) | copy-start | bytes 15364
  68.5 9.9 %copy-start.41 = (f32[4,320]{1,0:T(4,128)}, f32[4,320]{1,0:T(4,128)S(1)}, u32[]{:S(2)}) copy-start(f32[4,320]{1,0:T(4,128)S(1)} %mul.187) | copy-start | bytes 15364
  70.8 20.7 %copy-start.5 = (bf16[4,16,24,320]{3,2,1,0:T(8,128)(2,1)}, bf16[4,16,24,320]{3,2,1,0:T(8,128)(2,1)S(1)}, u32[]{:S(2)}) copy-start(bf16[4,16,24,320]{3,2,1,0:T(8,128)(2,1)S(1)} %fusion.17) | copy-start | bytes 2949124
  70.8 7.6 %collective-permute-start = (bf16[4,1,24,320]{3,2,1,0:T(8,128)(2,1)S(1)}, bf16[4,1,24,320]{3,2,1,0:T(8,128)(2,1)S(1)}, u32[]{:S(2)}, u32[]{:S(2)}) collective-permute-start(bf16[4,1,24,320]{3,2,1,0:T(8,128)(2,1)S(1)} %get-tuple-element.339), channel_id=1, source_target_pairs={{0,4},{4,8},{8,12},{1,5},{5,9},{9,13},{2,6},{6,10},{10,14},{3,7},{... | collective-permute-start | bytes 184328 | tf_op jit(solution)/shard_map/ppermute | solution.py:31
  74.5 6.2 %collective-permute-start.1 = (bf16[4,1,24,320]{3,2,1,0:T(8,128)(2,1)S(1)}, bf16[4,1,24,320]{3,2,1,0:T(8,128)(2,1)S(1)}, u32[]{:S(2)}, u32[]{:S(2)}) collective-permute-start(bf16[4,1,24,320]{3,2,1,0:T(8,128)(2,1)S(1)} %get-tuple-element.340), channel_id=1, source_target_pairs={{4,0},{8,4},{12,8},{5,1},{9,5},{13,9},{6,2},{10,6},{14,10},{7,3},{... | collective-permute-start | bytes 184328 | tf_op jit(solution)/shard_map/ppermute | solution.py:34
  78.4 13.1 %copy-start.32 = (bf16[4,1,24,320]{3,2,1,0:T(8,128)(2,1)}, bf16[4,1,24,320]{3,2,1,0:T(8,128)(2,1)S(1)}, u32[]{:S(2)}) copy-start(bf16[4,1,24,320]{3,2,1,0:T(8,128)(2,1)S(1)} %collective-permute-done) | copy-start | bytes 184324
  80.7 10.8 %copy-start.30 = (bf16[4,1,24,320]{3,2,1,0:T(8,128)(2,1)}, bf16[4,1,24,320]{3,2,1,0:T(8,128)(2,1)S(1)}, u32[]{:S(2)}) copy-start(bf16[4,1,24,320]{3,2,1,0:T(8,128)(2,1)S(1)} %collective-permute-done.1) | copy-start | bytes 184324
  80.9 7.7 %collective-permute-start.2 = (bf16[4,18,1,320]{3,2,1,0:T(2,128)(2,1)S(1)}, bf16[4,18,1,320]{3,2,1,0:T(2,128)(2,1)S(1)}, u32[]{:S(2)}, u32[]{:S(2)}) collective-permute-start(bf16[4,18,1,320]{3,2,1,0:T(2,128)(2,1)S(1)} %get-tuple-element.333), channel_id=1, source_target_pairs={{0,1},{1,2},{2,3},{4,5},{5,6},{6,7},{8,9},{9,10},{10,11},{12,13},{... | collective-permute-start | bytes 138248 | tf_op jit(solution)/shard_map/ppermute | solution.py:31
  84.8 6.6 %collective-permute-start.3 = (bf16[4,18,1,320]{3,2,1,0:T(2,128)(2,1)S(1)}, bf16[4,18,1,320]{3,2,1,0:T(2,128)(2,1)S(1)}, u32[]{:S(2)}, u32[]{:S(2)}) collective-permute-start(bf16[4,18,1,320]{3,2,1,0:T(2,128)(2,1)S(1)} %get-tuple-element.334), channel_id=1, source_target_pairs={{1,0},{2,1},{3,2},{5,4},{6,5},{7,6},{9,8},{10,9},{11,10},{13,12},{... | collective-permute-start | bytes 138248 | tf_op jit(solution)/shard_map/ppermute | solution.py:34
  92.6 10.8 %copy-start.13 = (bf16[4,18,25,320]{3,2,1,0:T(8,128)(2,1)}, bf16[4,18,25,320]{3,2,1,0:T(8,128)(2,1)S(1)}, u32[]{:S(2)}) copy-start(bf16[4,18,25,320]{3,2,1,0:T(8,128)(2,1)S(1)} %get-tuple-element.331) | copy-start | bytes 3456004
  114.5 230.3 %all-gather.8.cloned.1.call-start = ((), (), s32[]{:S(2)}) async-start(), calls=%async_computation.2 | async-start | bytes 5308416 | tf_op jit(solution)/shard_map/all_gather | solution.py:13
  114.9 18.0 %copy-start.7 = (bf16[4,16,24,320]{3,2,1,0:T(8,128)(2,1)}, bf16[4,16,24,320]{3,2,1,0:T(8,128)(2,1)S(1)}, u32[]{:S(2)}) copy-start(bf16[4,16,24,320]{3,2,1,0:T(8,128)(2,1)S(1)} %multiply_convert_fusion) | copy-start | bytes 2949124
  114.9 6.9 %collective-permute-start.8 = (bf16[4,1,24,320]{3,2,1,0:T(8,128)(2,1)S(1)}, bf16[4,1,24,320]{3,2,1,0:T(8,128)(2,1)S(1)}, u32[]{:S(2)}, u32[]{:S(2)}) collective-permute-start(bf16[4,1,24,320]{3,2,1,0:T(8,128)(2,1)S(1)} %get-tuple-element.336), channel_id=1, source_target_pairs={{0,4},{4,8},{8,12},{1,5},{5,9},{9,13},{2,6},{6,10},{10,14},{3,7},{... | collective-permute-start | bytes 184328 | tf_op jit(solution)/shard_map/ppermute | solution.py:31
  117.2 6.2 %collective-permute-start.9 = (bf16[4,1,24,320]{3,2,1,0:T(8,128)(2,1)S(1)}, bf16[4,1,24,320]{3,2,1,0:T(8,128)(2,1)S(1)}, u32[]{:S(2)}, u32[]{:S(2)}) collective-permute-start(bf16[4,1,24,320]{3,2,1,0:T(8,128)(2,1)S(1)} %get-tuple-element.335), channel_id=1, source_target_pairs={{4,0},{8,4},{12,8},{5,1},{9,5},{13,9},{6,2},{10,6},{14,10},{7,3},{... | collective-permute-start | bytes 184328 | tf_op jit(solution)/shard_map/ppermute | solution.py:34
  121.8 11.1 %copy-start.10 = (bf16[3,3,320,320]{3,2,1,0:T(8,128)(2,1)S(1)}, bf16[3,3,320,320]{3,2,1,0:T(8,128)(2,1)}, u32[]{:S(2)}) copy-start(bf16[3,3,320,320]{3,2,1,0:T(8,128)(2,1)} %param.24) | copy-start | bytes 5529604
  121.9 11.0 %copy-start.34 = (bf16[4,1,24,320]{3,2,1,0:T(8,128)(2,1)}, bf16[4,1,24,320]{3,2,1,0:T(8,128)(2,1)S(1)}, u32[]{:S(2)}) copy-start(bf16[4,1,24,320]{3,2,1,0:T(8,128)(2,1)S(1)} %collective-permute-done.8) | copy-start | bytes 184324
  123.5 9.4 %copy-start.36 = (bf16[4,1,24,320]{3,2,1,0:T(8,128)(2,1)}, bf16[4,1,24,320]{3,2,1,0:T(8,128)(2,1)S(1)}, u32[]{:S(2)}) copy-start(bf16[4,1,24,320]{3,2,1,0:T(8,128)(2,1)S(1)} %collective-permute-done.9) | copy-start | bytes 184324
  123.7 11.8 %collective-permute-start.10 = (bf16[4,18,1,320]{3,2,1,0:T(2,128)(2,1)S(1)}, bf16[4,18,1,320]{3,2,1,0:T(2,128)(2,1)S(1)}, u32[]{:S(2)}, u32[]{:S(2)}) collective-permute-start(bf16[4,18,1,320]{3,2,1,0:T(2,128)(2,1)S(1)} %get-tuple-element.326), channel_id=1, source_target_pairs={{1,0},{2,1},{3,2},{5,4},{6,5},{7,6},{9,8},{10,9},{11,10},{13,12},{... | collective-permute-start | bytes 138248 | tf_op jit(solution)/shard_map/ppermute | solution.py:34
  125.0 10.5 %collective-permute-start.11 = (bf16[4,18,1,320]{3,2,1,0:T(2,128)(2,1)S(1)}, bf16[4,18,1,320]{3,2,1,0:T(2,128)(2,1)S(1)}, u32[]{:S(2)}, u32[]{:S(2)}) collective-permute-start(bf16[4,18,1,320]{3,2,1,0:T(2,128)(2,1)S(1)} %get-tuple-element.325), channel_id=1, source_target_pairs={{0,1},{1,2},{2,3},{4,5},{5,6},{6,7},{8,9},{9,10},{10,11},{12,13},{... | collective-permute-start | bytes 138248 | tf_op jit(solution)/shard_map/ppermute | solution.py:31
  295.8 9.1 %copy-start.44 = (f32[4]{0:T(128)S(1)}, f32[4]{0:T(128)}, u32[]{:S(2)}) copy-start(f32[4]{0:T(128)} %param.19) | copy-start | bytes 52
  299.9 163.7 %all-reduce.9.cloned.1.call-start = ((), (), s32[]{:S(2)}) async-start(), calls=%async_computation.4 | async-start | bytes 11796480
  301.5 14.3 %collective-permute-start.4 = (bf16[4,1,24,320]{3,2,1,0:T(8,128)(2,1)}, bf16[4,1,24,320]{3,2,1,0:T(8,128)(2,1)}, u32[]{:S(2)}, u32[]{:S(2)}) collective-permute-start(bf16[4,1,24,320]{3,2,1,0:T(8,128)(2,1)} %get-tuple-element.337), channel_id=1, source_target_pairs={{0,4},{4,8},{8,12},{1,5},{5,9},{9,13},{2,6},{6,10},{10,14},{3,7},{... | collective-permute-start | bytes 184328 | tf_op jit(solution)/shard_map/ppermute | solution.py:31
  303.5 12.4 %collective-permute-start.5 = (bf16[4,1,24,320]{3,2,1,0:T(8,128)(2,1)}, bf16[4,1,24,320]{3,2,1,0:T(8,128)(2,1)}, u32[]{:S(2)}, u32[]{:S(2)}) collective-permute-start(bf16[4,1,24,320]{3,2,1,0:T(8,128)(2,1)} %get-tuple-element.338), channel_id=1, source_target_pairs={{4,0},{8,4},{12,8},{5,1},{9,5},{13,9},{6,2},{10,6},{14,10},{7,3},{... | collective-permute-start | bytes 184328 | tf_op jit(solution)/shard_map/ppermute | solution.py:34
  317.3 13.1 %collective-permute-start.6 = (bf16[4,18,1,320]{3,2,1,0:T(2,128)(2,1)S(1)}, bf16[4,18,1,320]{3,2,1,0:T(2,128)(2,1)S(1)}, u32[]{:S(2)}, u32[]{:S(2)}) collective-permute-start(bf16[4,18,1,320]{3,2,1,0:T(2,128)(2,1)S(1)} %get-tuple-element.329), channel_id=1, source_target_pairs={{0,1},{1,2},{2,3},{4,5},{5,6},{6,7},{8,9},{9,10},{10,11},{12,13},{... | collective-permute-start | bytes 138248 | tf_op jit(solution)/shard_map/ppermute | solution.py:31
  318.6 11.8 %collective-permute-start.7 = (bf16[4,18,1,320]{3,2,1,0:T(2,128)(2,1)S(1)}, bf16[4,18,1,320]{3,2,1,0:T(2,128)(2,1)S(1)}, u32[]{:S(2)}, u32[]{:S(2)}) collective-permute-start(bf16[4,18,1,320]{3,2,1,0:T(2,128)(2,1)S(1)} %get-tuple-element.330), channel_id=1, source_target_pairs={{1,0},{2,1},{3,2},{5,4},{6,5},{7,6},{9,8},{10,9},{11,10},{13,12},{... | collective-permute-start | bytes 138248 | tf_op jit(solution)/shard_map/ppermute | solution.py:34
  381.7 117.7 %all-gather.6.cloned.1.call-start = ((), (), s32[]{:S(2)}) async-start(), calls=%async_computation.1 | async-start | bytes 5308416 | tf_op jit(solution)/shard_map/all_gather | solution.py:13
  399.7 11.0 %copy-start.49 = (u32[128]{0:T(128)S(1)}, u32[128]{0:T(128)}, u32[]{:S(2)}) copy-start(u32[128]{0:T(128)} %constant.115) | copy-start | bytes 1540
  410.6 178.6 %all-reduce.7.cloned.1.call-start = ((), (), s32[]{:S(2)}) async-start(), calls=%async_computation.3 | async-start | bytes 1474560 | tf_op jit(solution)/shard_map/psum | solution.py:185
  508.1 83.0 %copy-start.1 = (f32[1000,320]{0,1:T(8,128)S(1)}, f32[1000,320]{0,1:T(8,128)}, u32[]{:S(2)}) copy-start(f32[1000,320]{0,1:T(8,128)} %param.22) | copy-start | bytes 3840004
  (35 other events, 116.5 us)
Sparse Core Ops, SparseCore 0:
  114.6 32.3 all-gather.3
  300.0 29.2 all-gather.7
  381.8 81.6 all-reduce.8
  465.2 34.1 all-gather.5
  502.9 86.2 all-reduce.6
